TPU v7x, 256 devices: a whole 4x4x8 slice. The times are simulated.
256 devices in a mesh: wide: 16 (over x, y), narrow: 16 (over z, core).
Axes of the slice: x: 4, y: 4, z: 8, core: 2. Of those that a mesh axis runs over, the one named last changes fastest.
Arguments:
- entries: int32 [65536, 32, 256], P(('wide', 'narrow')), may hold values from 0 to 2
- factor_a: float32 [131072, 128], P(('wide', 'narrow')), may hold values from -4.2 to 4.2
- factor_b: float32 [131072, 128], P(('wide', 'narrow')), may hold values from -4.2 to 4.2
- factor_c: float32 [8192, 128], P('wide'), may hold values from -4.2 to 4.2
- index_a: int32 [65536], P(('wide', 'narrow')), may hold values from 0 to 511
- index_b: int32 [65536], P(('wide', 'narrow')), may hold values from 0 to 511
- index_c: int32 [8192], P(('wide', 'narrow')), may hold values from 0 to 511
Outputs:
- step_a: float32 [131072, 128], P(('wide', 'narrow'))
- step_b: float32 [131072, 128], P(('wide', 'narrow'))
- step_c: float32 [8192, 128], P('wide')
All inputs are finite; a program needn't handle non-finite values.
Results may differ from a plain program's by a relative error of at most 0.0048.
Values may be sent and summed in bfloat16 or wider, within the bound.
No kernel may reach another device: no remote copies, remote signals or barrier semaphores. Data moves between devices by JAX's collectives and lax.ppermute only.
A program may use at most 128 MiB of HBM per device.

v0:
```python
import jax
import jax.numpy as jnp
from jax import lax
from jax.sharding import PartitionSpec as P

CG_ITERS = 2
ridge_weight = 25.0


def outer_pairs(rows_first, rows_third):
    product = (
        rows_first.astype(jnp.float32)[:, None, :] * rows_third.astype(jnp.float32)[None, :, :]
    )
    return product.astype(jnp.bfloat16).reshape(-1, rows_first.shape[1])


def model_values(pairs, rows_second):
    return lax.dot_general(
        pairs, rows_second, (((1,), (1,)), ((), ())), preferred_element_type=jnp.float32
    )


def fisher_terms(model, codes):
    sampled = (codes > 0).astype(jnp.float32)
    present = (codes == 2).astype(jnp.float32)
    prob = jax.nn.sigmoid(model)
    weight = sampled * prob * (1.0 - prob)
    slope = (sampled * (prob - present)).astype(jnp.bfloat16)
    return (weight, slope)


def transposed(upstream, pairs, rows_first, rows_second, rows_third):
    over = jnp.dot(upstream, rows_second, preferred_element_type=jnp.float32)
    over = over.reshape(rows_first.shape[0], rows_third.shape[0], -1)
    to_first = jnp.sum(over * rows_third.astype(jnp.float32)[None, :, :], axis=1)
    to_third = jnp.sum(over * rows_first.astype(jnp.float32)[:, None, :], axis=0)
    to_second = lax.dot_general(
        upstream, pairs, (((0,), (0,)), ((), ())), preferred_element_type=jnp.float32
    )
    return (to_first, to_second, to_third)


def add_scaled(base_set, factor, extra_set):
    return (
        base_set[0] + factor * extra_set[0],
        base_set[1] + factor * extra_set[1],
        base_set[2] + factor * extra_set[2],
    )


def local(entries, factor_a, factor_b, factor_c, index_a, index_b, index_c):
    wide_count = lax.axis_size("wide")
    narrow_count = lax.axis_size("narrow")
    block_first, block_third, block_second = entries.shape
    slots_a = block_first // wide_count
    slots_b = block_second // narrow_count
    slots_c = block_third // wide_count
    codes = entries.reshape(block_first * block_third, block_second)
    c_weight = (lax.axis_index("narrow") == 0).astype(jnp.float32)

    def tube_total(partial_value):
        return lax.psum(partial_value, "narrow")

    def fetch(table_a, table_b, table_c):
        send_a = table_a[index_a].astype(jnp.bfloat16).reshape(wide_count, slots_a, -1)
        send_c = table_c[index_c].astype(jnp.bfloat16).reshape(wide_count, slots_c, -1)
        got_a, got_c = (
            lax.all_to_all(send_a, "wide", split_axis=0, concat_axis=0, tiled=True),
            lax.all_to_all(send_c, "wide", split_axis=0, concat_axis=0, tiled=True),
        )
        send_b = table_b[index_b].astype(jnp.bfloat16).reshape(narrow_count, slots_b, -1)
        got_b = lax.all_to_all(send_b, "narrow", split_axis=0, concat_axis=0, tiled=True)
        return (
            got_a.reshape(block_first, -1),
            got_b.reshape(block_second, -1),
            got_c.reshape(block_third, -1),
        )

    def give_back(parts, field):
        back_a, back_c = (
            lax.all_to_all(
                parts[0].reshape(wide_count, slots_a, -1),
                "wide",
                split_axis=0,
                concat_axis=0,
                tiled=True,
            ),
            lax.all_to_all(
                parts[2].reshape(wide_count, slots_c, -1),
                "wide",
                split_axis=0,
                concat_axis=0,
                tiled=True,
            ),
        )
        back_b = lax.all_to_all(
            parts[1].reshape(narrow_count, slots_b, -1),
            "narrow",
            split_axis=0,
            concat_axis=0,
            tiled=True,
        )
        sum_a = (
            jnp.zeros(factor_a.shape, jnp.float32).at[index_a].add(back_a.reshape(block_first, -1))
        )
        sum_b = (
            jnp.zeros(factor_b.shape, jnp.float32).at[index_b].add(back_b.reshape(block_second, -1))
        )
        part_c = (
            jnp.zeros(factor_c.shape, jnp.float32).at[index_c].add(back_c.reshape(block_third, -1))
        )
        sum_c = tube_total(part_c)
        return (
            sum_a + ridge_weight * field[0],
            sum_b + ridge_weight * field[1],
            sum_c + ridge_weight * field[2],
        )

    rows_first, rows_second, rows_third = fetch(factor_a, factor_b, factor_c)
    pairs = outer_pairs(rows_first, rows_third)
    weight, slope = fisher_terms(model_values(pairs, rows_second), codes)
    gradient = give_back(
        transposed(slope, pairs, rows_first, rows_second, rows_third),
        (factor_a, factor_b, factor_c),
    )

    def local_inner(first_set, second_set):
        return (
            jnp.sum(first_set[0] * second_set[0])
            + jnp.sum(first_set[1] * second_set[1])
            + c_weight * jnp.sum(first_set[2] * second_set[2])
        )

    def squares(vector_set):
        return lax.psum(local_inner(vector_set, vector_set), ("wide", "narrow"))

    solution = (
        jnp.zeros_like(gradient[0]),
        jnp.zeros_like(gradient[1]),
        jnp.zeros_like(gradient[2]),
    )
    residual = add_scaled(solution, -1.0, gradient)
    direction = residual
    norm_now = squares(residual)
    for iteration in range(CG_ITERS):
        d_first, d_second, d_third = fetch(direction[0], direction[1], direction[2])
        mixed = d_first.astype(jnp.float32)[:, None, :] * rows_third.astype(jnp.float32)[None, :, :]
        mixed = (
            mixed
            + rows_first.astype(jnp.float32)[:, None, :] * d_third.astype(jnp.float32)[None, :, :]
        )
        mixed = mixed.astype(jnp.bfloat16).reshape(block_first * block_third, -1)
        change = model_values(mixed, rows_second) + model_values(pairs, d_second)
        scaled = (weight * change).astype(jnp.bfloat16)
        image = give_back(transposed(scaled, pairs, rows_first, rows_second, rows_third), direction)
        alpha = norm_now / lax.psum(local_inner(direction, image), ("wide", "narrow"))
        solution = add_scaled(solution, alpha, direction)
        residual = add_scaled(residual, -alpha, image)
        if iteration + 1 < CG_ITERS:
            norm_next = squares(residual)
            direction = add_scaled(residual, norm_next / norm_now, direction)
            norm_now = norm_next
    return (solution[0], solution[1], solution[2])


def solution(mesh):
    placed = (
        P(("wide", "narrow"), None, None),
        P(("wide", "narrow"), None),
        P(("wide", "narrow"), None),
        P("wide", None),
        P(("wide", "narrow")),
        P(("wide", "narrow")),
        P(("wide", "narrow")),
    )
    return jax.shard_map(
        local,
        mesh=mesh,
        in_specs=placed,
        out_specs=(P(("wide", "narrow"), None), P(("wide", "narrow"), None), P("wide", None)),
        check_vma=False,
    )
```

profile of v0, /device:TPU:1, one launch (start us, length us, event | category | flops | bytes accessed | tf_op | source)
XLA Modules:
  0.0 847.4 jit_solution(3459871042274869847)
XLA Ops:
  10.0 7.6 all-to-all-start.1
  18.9 7.4 broadcast_compare_fusion
  27.7 6.7 all-to-all-start
  35.8 5.1 all-to-all-done
  40.9 11.1 %all-to-all-start.2 = ((bf16[16,16,128]{2,1,0:T(8,128)(2,1)}), bf16[16,16,128]{2,1,0:T(8,128)(2,1)S(1)}, u32[]{:S(2)}, u32[]{:S(2)}) async-start(bf16[16,16,128]{2,1,0:T(8,128)(2,1)} %bitcast.6), calls=%async_computation.2 | async-start | bytes 131072 | tf_op jit(solution)/shard_map/all_to_all | solution.py:72
  54.0 5.9 all-to-all-done.2
  59.8 8.6 %subtract_multiply_fusion = (f32[8192,256]{1,0:T(8,128)}, bf16[8192,256]{1,0:T(8,128)(2,1)S(1)}) fusion(pred[256,32,256]{2,1,0:T(32,128)(4,1)} %get-tuple-element.25, f32[256,32,256]{2,1,0:T(8,128)} %get-tuple-element.26, bf16[8192,128]{1,0:T(8,128)(2,1)S(1)} %bitcast.86, bf16[256,128]{1,0:T(8,128)(2,1)S(1)} %bitcast.103), kind=kOutput, calls=%fused_computation.31 | convolution fusion | flops 555745280 | bytes 25231360 | tf_op jit(solution)/shard_map/dot_general | solution.py:18
  68.4 5.7 multiply_reduce_fusion.4
  77.7 6.3 all-to-all-done.5
  89.6 6.4 copy.18
  98.0 99.5 %all-reduce.5.cloned.1.call-done = f32[512,128]{1,0:T(8,128)} async-done(((f32[512,128]{1,0:T(8,128)}), f32[512,128]{1,0:T(8,128)}) %all-reduce.5.cloned.1.call-update) | async-done | bytes 262160 | tf_op jit(solution)/shard_map/psum | solution.py:62
  199.7 6.5 all-to-all-start.7
  207.7 4.8 all-to-all-done.7
  222.5 9.3 %all-to-all-start.4 = ((f32[16,16,128]{2,1,0:T(8,128)}), f32[16,16,128]{2,1,0:T(8,128)S(1)}, u32[]{:S(2)}, u32[]{:S(2)}) async-start(f32[16,16,128]{2,1,0:T(8,128)} %fusion.21), calls=%async_computation.4 | async-start | bytes 262144 | tf_op jit(solution)/shard_map/all_to_all | solution.py:96
  235.2 5.8 all-to-all-done.4
  248.3 6.1 fusion.22
  255.6 7.0 fusion.4
  262.6 5.7 multiply_reduce_fusion.2
  271.9 6.4 copy.21
  278.2 6.6 all-to-all-start.9
  292.3 7.6 all-to-all-start.10
  302.3 97.3 %all-reduce.7.cloned.1.call-done = f32[512,128]{1,0:T(8,128)} async-done(((f32[512,128]{1,0:T(8,128)}), f32[512,128]{1,0:T(8,128)}) %all-reduce.7.cloned.1.call-update) | async-done | bytes 262160 | tf_op jit(solution)/shard_map/psum | solution.py:62
  408.3 77.7 %all-reduce = (f32[]{:T(128)}, f32[]{:T(128)}) all-reduce(f32[]{:T(128)S(6)} %add.165, f32[]{:T(128)S(6)} %add.170), channel_id=1, replica_groups=mesh['wide'=16,'narrow'=16] {'wide','narrow'}, use_global_device_ids=true, to_apply=%region_9.0 | all-reduce | flops 2 | bytes 16 | tf_op jit(solution)/shard_map/psum | solution.py:135
  492.2 72.2 %psum.53 = f32[]{:T(128)} all-reduce(f32[]{:T(128)S(6)} %add.175), channel_id=1, replica_groups=mesh['wide'=16,'narrow'=16] {'wide','narrow'}, use_global_device_ids=true, to_apply=%region_23.0 | all-reduce | flops 1 | bytes 8 | tf_op jit(solution)/shard_map/psum | solution.py:135
  590.8 7.9 all-to-all-start.14
  606.7 7.0 fusion.5
  613.8 5.7 multiply_reduce_fusion
  623.2 6.4 copy.24
  629.6 6.6 all-to-all-start.15
  643.0 9.1 %all-to-all-start.16 = ((f32[16,16,128]{2,1,0:T(8,128)}), f32[16,16,128]{2,1,0:T(8,128)S(1)}, u32[]{:S(2)}, u32[]{:S(2)}) async-start(f32[16,16,128]{2,1,0:T(8,128)} %fusion.25), calls=%async_computation.16 | async-start | bytes 262144 | tf_op jit(solution)/shard_map/all_to_all | solution.py:96
  654.9 98.0 %all-reduce.9.cloned.1.call-done = f32[512,128]{1,0:T(8,128)} async-done(((f32[512,128]{1,0:T(8,128)}), f32[512,128]{1,0:T(8,128)}) %all-reduce.9.cloned.1.call-update) | async-done | bytes 262160 | tf_op jit(solution)/shard_map/psum | solution.py:62
  759.2 77.7 %psum.55 = f32[]{:T(128)} all-reduce(f32[]{:T(128)S(6)} %add.183), channel_id=1, replica_groups=mesh['wide'=16,'narrow'=16] {'wide','narrow'}, use_global_device_ids=true, to_apply=%region_33.0 | all-reduce | flops 1 | bytes 8 | tf_op jit(solution)/shard_map/psum | solution.py:156
  (136 shorter events, 119.3 us)
Async XLA Ops:
  7.8 80.3 %copy-start.23 = (s32[32]{0:T(128)}, s32[32]{0:T(128)S(1)}, u32[]{:S(2)}) copy-start(s32[32]{0:T(128)S(1)} %compare_select_fusion.2) | copy-start | bytes 388
  7.8 190.7 %copy-start.22 = (s32[1024]{0:T(1024)}, s32[1024]{0:T(1024)S(1)}, u32[]{:S(2)}) copy-start(s32[1024]{0:T(1024)S(1)} %pad_clamp_fusion.1) | copy-start | bytes 12292
  10.0 17.7 %all-to-all-start.1 = ((bf16[16,2,128]{2,1,0:T(2,128)(2,1)}), bf16[16,2,128]{2,1,0:T(2,128)(2,1)S(1)}, u32[]{:S(2)}, u32[]{:S(2)}) async-start(bf16[16,2,128]{2,1,0:T(2,128)(2,1)} %bitcast.3), calls=%async_computation.1 | async-start | bytes 16384 | tf_op jit(solution)/shard_map/all_to_all | solution.py:69
  18.2 77.7 %copy-start.17 = (s32[256]{0:T(256)}, s32[256]{0:T(256)S(1)}, u32[]{:S(2)}) copy-start(s32[256]{0:T(256)S(1)} %compare_select_fusion.1) | copy-start | bytes 3076
  26.3 179.9 %copy-start.21 = (s32[1024]{0:T(1024)}, s32[1024]{0:T(1024)S(1)}, u32[]{:S(2)}) copy-start(s32[1024]{0:T(1024)S(1)} %pad_clamp_fusion.2) | copy-start | bytes 12292
  27.7 13.2 %all-to-all-start = ((bf16[16,16,128]{2,1,0:T(8,128)(2,1)}), bf16[16,16,128]{2,1,0:T(8,128)(2,1)S(1)}, u32[]{:S(2)}, u32[]{:S(2)}) async-start(bf16[16,16,128]{2,1,0:T(8,128)(2,1)} %bitcast.1), calls=%async_computation | async-start | bytes 131072 | tf_op jit(solution)/shard_map/all_to_all | solution.py:68
  40.9 19.0 %all-to-all-start.2 = ((bf16[16,16,128]{2,1,0:T(8,128)(2,1)}), bf16[16,16,128]{2,1,0:T(8,128)(2,1)S(1)}, u32[]{:S(2)}, u32[]{:S(2)}) async-start(bf16[16,16,128]{2,1,0:T(8,128)(2,1)} %bitcast.6), calls=%async_computation.2 | async-start | bytes 131072 | tf_op jit(solution)/shard_map/all_to_all | solution.py:72
  59.8 202.8 %copy-start.10 = (bf16[16,16,128]{2,1,0:T(8,128)(2,1)}, bf16[16,16,128]{2,1,0:T(8,128)(2,1)S(1)}, u32[]{:S(2)}) copy-start(bf16[16,16,128]{2,1,0:T(8,128)(2,1)S(1)} %all-to-all-done.2) | copy-start | bytes 196612
  74.1 9.9 %all-to-all-start.5 = ((f32[16,2,128]{2,1,0:T(2,128)}), f32[16,2,128]{2,1,0:T(2,128)S(1)}, u32[]{:S(2)}, u32[]{:S(2)}) async-start(f32[16,2,128]{2,1,0:T(2,128)} %bitcast.17), calls=%async_computation.5 | async-start | bytes 32768 | tf_op jit(solution)/shard_map/all_to_all | solution.py:88
  84.0 11.9 %all-to-all-start.3 = ((f32[16,16,128]{2,1,0:T(8,128)}), f32[16,16,128]{2,1,0:T(8,128)S(1)}, u32[]{:S(2)}, u32[]{:S(2)}) async-start(f32[16,16,128]{2,1,0:T(8,128)} %bitcast.11), calls=%async_computation.3 | async-start | bytes 262144 | tf_op jit(solution)/shard_map/all_to_all | solution.py:81
  87.5 110.0 %all-reduce.5.cloned.1.call-start = ((), (), s32[]{:S(2)}) async-start(), calls=%async_computation.18 | async-start | bytes 524288 | tf_op jit(solution)/shard_map/psum | solution.py:62
  89.6 107.9 %copy-start.13 = (f32[512,128]{1,0:T(8,128)S(1)}, f32[512,128]{1,0:T(8,128)}, u32[]{:S(2)}) copy-start(f32[512,128]{1,0:T(8,128)} %param.10) | copy-start | bytes 786436
  198.5 367.3 %copy-start.3 = (f32[512,128]{1,0:T(8,128)}, f32[512,128]{1,0:T(8,128)S(1)}, u32[]{:S(2)}) copy-start(f32[512,128]{1,0:T(8,128)S(1)} %get-tuple-element.22) | copy-start | bytes 786436
  199.7 12.9 %all-to-all-start.7 = ((bf16[16,2,128]{2,1,0:T(2,128)(2,1)}), bf16[16,2,128]{2,1,0:T(2,128)(2,1)S(1)}, u32[]{:S(2)}, u32[]{:S(2)}) async-start(bf16[16,2,128]{2,1,0:T(2,128)(2,1)} %bitcast.21), calls=%async_computation.7 | async-start | bytes 16384 | tf_op jit(solution)/shard_map/all_to_all | solution.py:69
  212.6 10.0 %all-to-all-start.6 = ((bf16[16,16,128]{2,1,0:T(8,128)(2,1)}), bf16[16,16,128]{2,1,0:T(8,128)(2,1)S(1)}, u32[]{:S(2)}, u32[]{:S(2)}) async-start(bf16[16,16,128]{2,1,0:T(8,128)(2,1)} %bitcast.19), calls=%async_computation.6 | async-start | bytes 131072 | tf_op jit(solution)/shard_map/all_to_all | solution.py:68
  222.5 18.5 %all-to-all-start.4 = ((f32[16,16,128]{2,1,0:T(8,128)}), f32[16,16,128]{2,1,0:T(8,128)S(1)}, u32[]{:S(2)}, u32[]{:S(2)}) async-start(f32[16,16,128]{2,1,0:T(8,128)} %fusion.21), calls=%async_computation.4 | async-start | bytes 262144 | tf_op jit(solution)/shard_map/all_to_all | solution.py:96
  244.7 10.8 %all-to-all-start.8 = ((bf16[16,16,128]{2,1,0:T(8,128)(2,1)}), bf16[16,16,128]{2,1,0:T(8,128)(2,1)S(1)}, u32[]{:S(2)}, u32[]{:S(2)}) async-start(bf16[16,16,128]{2,1,0:T(8,128)(2,1)} %bitcast.24), calls=%async_computation.8 | async-start | bytes 131072 | tf_op jit(solution)/shard_map/all_to_all | solution.py:72
  268.3 9.9 %all-to-all-start.11 = ((f32[16,2,128]{2,1,0:T(2,128)}), f32[16,2,128]{2,1,0:T(2,128)S(1)}, u32[]{:S(2)}, u32[]{:S(2)}) async-start(f32[16,2,128]{2,1,0:T(2,128)} %bitcast.34), calls=%async_computation.11 | async-start | bytes 32768 | tf_op jit(solution)/shard_map/all_to_all | solution.py:88
  278.2 13.3 %all-to-all-start.9 = ((f32[16,16,128]{2,1,0:T(8,128)}), f32[16,16,128]{2,1,0:T(8,128)S(1)}, u32[]{:S(2)}, u32[]{:S(2)}) async-start(f32[16,16,128]{2,1,0:T(8,128)} %bitcast.28), calls=%async_computation.9 | async-start | bytes 262144 | tf_op jit(solution)/shard_map/all_to_all | solution.py:81
  284.8 114.7 %all-reduce.7.cloned.1.call-start = ((), (), s32[]{:S(2)}) async-start(), calls=%async_computation.19 | async-start | bytes 524288 | tf_op jit(solution)/shard_map/psum | solution.py:62
  292.3 110.2 %all-to-all-start.10 = ((f32[16,16,128]{2,1,0:T(8,128)}), f32[16,16,128]{2,1,0:T(8,128)}, u32[]{:S(2)}, u32[]{:S(2)}) async-start(f32[16,16,128]{2,1,0:T(8,128)} %fusion.23), calls=%async_computation.10 | async-start | bytes 262144 | tf_op jit(solution)/shard_map/all_to_all | solution.py:96
  569.7 10.4 %all-to-all-start.13 = ((bf16[16,2,128]{2,1,0:T(2,128)(2,1)}), bf16[16,2,128]{2,1,0:T(2,128)(2,1)}, u32[]{:S(2)}, u32[]{:S(2)}) async-start(bf16[16,2,128]{2,1,0:T(2,128)(2,1)} %bitcast.38), calls=%async_computation.13 | async-start | bytes 16384 | tf_op jit(solution)/shard_map/all_to_all | solution.py:69
  580.2 10.7 %all-to-all-start.12 = ((bf16[16,16,128]{2,1,0:T(8,128)(2,1)}), bf16[16,16,128]{2,1,0:T(8,128)(2,1)}, u32[]{:S(2)}, u32[]{:S(2)}) async-start(bf16[16,16,128]{2,1,0:T(8,128)(2,1)} %bitcast.36), calls=%async_computation.12 | async-start | bytes 131072 | tf_op jit(solution)/shard_map/all_to_all | solution.py:68
  590.8 15.9 %all-to-all-start.14 = ((bf16[16,16,128]{2,1,0:T(8,128)(2,1)}), bf16[16,16,128]{2,1,0:T(8,128)(2,1)S(1)}, u32[]{:S(2)}, u32[]{:S(2)}) async-start(bf16[16,16,128]{2,1,0:T(8,128)(2,1)} %bitcast.41), calls=%async_computation.14 | async-start | bytes 131072 | tf_op jit(solution)/shard_map/all_to_all | solution.py:72
  619.5 10.1 %all-to-all-start.17 = ((f32[16,2,128]{2,1,0:T(2,128)}), f32[16,2,128]{2,1,0:T(2,128)S(1)}, u32[]{:S(2)}, u32[]{:S(2)}) async-start(f32[16,2,128]{2,1,0:T(2,128)} %bitcast.49), calls=%async_computation.17 | async-start | bytes 32768 | tf_op jit(solution)/shard_map/all_to_all | solution.py:88
  629.6 13.4 %all-to-all-start.15 = ((f32[16,16,128]{2,1,0:T(8,128)}), f32[16,16,128]{2,1,0:T(8,128)S(1)}, u32[]{:S(2)}, u32[]{:S(2)}) async-start(f32[16,16,128]{2,1,0:T(8,128)} %bitcast.44), calls=%async_computation.15 | async-start | bytes 262144 | tf_op jit(solution)/shard_map/all_to_all | solution.py:81
  636.2 116.6 %all-reduce.9.cloned.1.call-start = ((), (), s32[]{:S(2)}) async-start(), calls=%async_computation.20 | async-start | bytes 524288 | tf_op jit(solution)/shard_map/psum | solution.py:62
  636.3 118.9 %copy-start.16 = (s32[256]{0:T(256)S(1)}, s32[256]{0:T(256)}, u32[]{:S(2)}) copy-start(s32[256]{0:T(256)} %copy-done.14) | copy-start | bytes 3076
  640.4 116.8 %copy-start.5 = (f32[512,128]{1,0:T(8,128)S(1)}, f32[512,128]{1,0:T(8,128)}, u32[]{:S(2)}) copy-start(f32[512,128]{1,0:T(8,128)} %get-tuple-element.18) | copy-start | bytes 786436
  640.4 198.6 %copy-start.4 = (f32[512,128]{1,0:T(8,128)S(1)}, f32[512,128]{1,0:T(8,128)}, u32[]{:S(2)}) copy-start(f32[512,128]{1,0:T(8,128)} %copy-done.3) | copy-start | bytes 786436
  640.4 198.6 %copy-start.7 = (f32[512,128]{1,0:T(8,128)S(1)}, f32[512,128]{1,0:T(8,128)}, u32[]{:S(2)}) copy-start(f32[512,128]{1,0:T(8,128)} %multiply_add_fusion.4) | copy-start | bytes 786436
  643.0 112.1 %all-to-all-start.16 = ((f32[16,16,128]{2,1,0:T(8,128)}), f32[16,16,128]{2,1,0:T(8,128)S(1)}, u32[]{:S(2)}, u32[]{:S(2)}) async-start(f32[16,16,128]{2,1,0:T(8,128)} %fusion.25), calls=%async_computation.16 | async-start | bytes 262144 | tf_op jit(solution)/shard_map/all_to_all | solution.py:96
  (13 other events, 141.1 us)
Sparse Core Ops, SparseCore 0:
  91.3 106.1 all-reduce.4
  290.6 108.8 all-reduce.6
  642.2 110.5 all-reduce.8
where the time goes:
time: 858 us; the launch traced here: 847 us
  waiting for transfers between devices  334 us (39%)
  blocking collectives  228 us (27%)
  starting transfers between devices  109 us (13%)
  matrix products  62.6 us (7%)
  other arithmetic  46.5 us (5%)
  local copies, waits for them, and re-layouts  41.5 us (5%)
  between operations  26.4 us (3%)
    psum x3, waiting for transfers between devices, tube_total(): return lax.psum(partial_value, 'narrow')  295 us
    psum x2, blocking collectives, squares(): return lax.psum(local_inner(vector_set, vector_set), ('wide', 'narrow'))  150 us
    psum x1, blocking collectives, local(): lax.psum(local_inner(direction, image), ('wide', 'narrow'))  77.7 us
    dot_general x5, matrix products, model_values(): lax.dot_general(pairs, rows_second, (((1,), (1,)), ((), ())), preferred_e...  33.1 us
    all_to_all x3, starting transfers between devices, give_back(): lax.all_to_all(parts[1].reshape(narrow_count, slots_b, -1), 'narrow', spl...  26 us
    all_to_all x3, starting transfers between devices, fetch(): lax.all_to_all(send_b, 'narrow', split_axis=0, concat_axis=0, tiled=True)  22.6 us
    dot_general x3, local copies, waits for them, and re-layouts, transposed(): lax.dot_general(upstream, pairs, (((0,), (0,)), ((), ())), preferred_elem...  19.2 us
    all_to_all x3, starting transfers between devices, fetch(): lax.all_to_all(send_c, 'wide', split_axis=0, concat_axis=0, tiled=True)  18.2 us
  transfers between devices with their start and end apart: 21, of which 15 were waited for; matrix products, arithmetic and copies ran while one was open for 10% of the time, Pallas kernels for 0%

commit v1 on v0

--- a/solution.py
+++ b/solution.py
@@ -5,6 +5,7 @@
 
 CG_ITERS = 2
 ridge_weight = 25.0
+divide_knots_on_mesh = lambda s0: lax.psum(lax.psum(s0, "wide"), "narrow")
 
 
 def outer_pairs(rows_first, rows_third):
@@ -132,7 +133,7 @@
         )
 
     def squares(vector_set):
-        return lax.psum(local_inner(vector_set, vector_set), ("wide", "narrow"))
+        return divide_knots_on_mesh(local_inner(vector_set, vector_set))
 
     solution = (
         jnp.zeros_like(gradient[0]),

time: 858 us -> 909 us (1.059)
  blocking collectives: 228 us -> 277 us
    psum x1 -> x2, blocking collectives: 77.7 us -> 150 us  [local(): lax.psum(local_inner(direction, image), ('wide', 'narrow'))]
    psum x2 -> x4, blocking collectives: 150 us -> 127 us  [divide_knots_on_mesh = lambda s0: lax.psum(lax.psum(s0, 'wide'), 'narrow')]
where the time goes in v1:
time: 909 us; the launch traced here: 898 us
  waiting for transfers between devices  334 us (37%)
  blocking collectives  277 us (30%)
  starting transfers between devices  110 us (12%)
  matrix products  62.6 us (7%)
  other arithmetic  46.6 us (5%)
  local copies, waits for them, and re-layouts  41.5 us (5%)
  between operations  26.4 us (3%)
    psum x3, waiting for transfers between devices, tube_total(): return lax.psum(partial_value, 'narrow')  295 us
    psum x2, blocking collectives, local(): lax.psum(local_inner(direction, image), ('wide', 'narrow'))  150 us
    psum x4, blocking collectives, divide_knots_on_mesh = lambda s0: lax.psum(lax.psum(s0, 'wide'), 'narrow')  127 us
    dot_general x5, matrix products, model_values(): lax.dot_general(pairs, rows_second, (((1,), (1,)), ((), ())), preferred_e...  33.1 us
    all_to_all x3, starting transfers between devices, give_back(): lax.all_to_all(parts[1].reshape(narrow_count, slots_b, -1), 'narrow', spl...  26 us
    all_to_all x3, starting transfers between devices, fetch(): lax.all_to_all(send_b, 'narrow', split_axis=0, concat_axis=0, tiled=True)  23.5 us
    dot_general x3, local copies, waits for them, and re-layouts, transposed(): lax.dot_general(upstream, pairs, (((0,), (0,)), ((), ())), preferred_elem...  19.2 us
    all_to_all x3, starting transfers between devices, fetch(): lax.all_to_all(send_c, 'wide', split_axis=0, concat_axis=0, tiled=True)  18.2 us
  transfers between devices with their start and end apart: 21, of which 15 were waited for; matrix products, arithmetic and copies ran while one was open for 10% of the time, Pallas kernels for 0%

profile of v1, /device:TPU:1, one launch (start us, length us, event | category | flops | bytes accessed | tf_op | source)
XLA Modules:
  0.0 898.1 jit_solution(14947684089069232221)
XLA Ops:
  10.0 7.6 all-to-all-start.1
  18.9 7.4 broadcast_compare_fusion
  27.7 6.7 all-to-all-start
  40.9 11.1 %all-to-all-start.2 = ((bf16[16,16,128]{2,1,0:T(8,128)(2,1)}), bf16[16,16,128]{2,1,0:T(8,128)(2,1)S(1)}, u32[]{:S(2)}, u32[]{:S(2)}) async-start(bf16[16,16,128]{2,1,0:T(8,128)(2,1)} %bitcast.6), calls=%async_computation.2 | async-start | bytes 131072 | tf_op jit(solution)/shard_map/all_to_all | solution.py:73
  54.0 5.9 all-to-all-done.2
  59.8 8.6 subtract_multiply_fusion
  68.4 5.7 multiply_reduce_fusion.4
  77.7 6.3 all-to-all-done.5
  89.6 6.4 copy.18
  98.0 99.5 %all-reduce.4.cloned.1.call-done = f32[512,128]{1,0:T(8,128)} async-done(((f32[512,128]{1,0:T(8,128)}), f32[512,128]{1,0:T(8,128)}) %all-reduce.4.cloned.1.call-update) | async-done | bytes 262160 | tf_op jit(solution)/shard_map/psum | solution.py:63
  199.7 6.5 all-to-all-start.7
  222.5 9.3 %all-to-all-start.4 = ((f32[16,16,128]{2,1,0:T(8,128)}), f32[16,16,128]{2,1,0:T(8,128)S(1)}, u32[]{:S(2)}, u32[]{:S(2)}) async-start(f32[16,16,128]{2,1,0:T(8,128)} %fusion.21), calls=%async_computation.4 | async-start | bytes 262144 | tf_op jit(solution)/shard_map/all_to_all | solution.py:97
  235.2 5.8 all-to-all-done.4
  248.3 6.1 fusion.22
  255.6 7.0 fusion.4
  271.9 6.4 copy.21
  278.2 6.6 all-to-all-start.9
  292.3 7.6 all-to-all-start.10
  302.3 97.3 %all-reduce.6.cloned.1.call-done = f32[512,128]{1,0:T(8,128)} async-done(((f32[512,128]{1,0:T(8,128)}), f32[512,128]{1,0:T(8,128)}) %all-reduce.6.cloned.1.call-update) | async-done | bytes 262160 | tf_op jit(solution)/shard_map/psum | solution.py:63
  407.0 33.6 %psum.64 = f32[]{:T(128)} all-reduce(f32[]{:T(128)S(6)} %add.169), channel_id=1, replica_groups=mesh['wide'=16,'narrow'=16] {'wide'}, use_global_device_ids=true, to_apply=%region_9.0 | all-reduce | flops 1 | bytes 8 | tf_op jit(solution)/shard_map/psum | solution.py:8
  441.9 31.4 %psum.65 = f32[]{:T(128)} all-reduce(f32[]{:T(128)} %psum.64), channel_id=1, replica_groups=mesh['wide'=16,'narrow'=16] {'narrow'}, use_global_device_ids=true, to_apply=%region_10.0 | all-reduce | flops 1 | bytes 8 | tf_op jit(solution)/shard_map/psum | solution.py:8
  473.3 72.7 %psum.67 = f32[]{:T(128)} all-reduce(f32[]{:T(128)S(6)} %add.174), channel_id=1, replica_groups=mesh['wide'=16,'narrow'=16] {'wide','narrow'}, use_global_device_ids=true, to_apply=%region_20.0 | all-reduce | flops 1 | bytes 8 | tf_op jit(solution)/shard_map/psum | solution.py:157
  552.2 30.3 %psum.68 = f32[]{:T(128)} all-reduce(f32[]{:T(128)S(6)} %add.179), channel_id=1, replica_groups=mesh['wide'=16,'narrow'=16] {'wide'}, use_global_device_ids=true, to_apply=%region_24.0 | all-reduce | flops 1 | bytes 8 | tf_op jit(solution)/shard_map/psum | solution.py:8
  582.5 31.7 %psum.69 = f32[]{:T(128)} all-reduce(f32[]{:T(128)} %psum.68), channel_id=1, replica_groups=mesh['wide'=16,'narrow'=16] {'narrow'}, use_global_device_ids=true, to_apply=%region_25.0 | all-reduce | flops 1 | bytes 8 | tf_op jit(solution)/shard_map/psum | solution.py:8
  640.6 8.7 all-to-all-start.14
  657.4 7.0 fusion.5
  664.4 5.7 multiply_reduce_fusion
  673.8 6.4 copy.24
  680.2 6.6 all-to-all-start.15
  693.7 9.1 %all-to-all-start.16 = ((f32[16,16,128]{2,1,0:T(8,128)}), f32[16,16,128]{2,1,0:T(8,128)S(1)}, u32[]{:S(2)}, u32[]{:S(2)}) async-start(f32[16,16,128]{2,1,0:T(8,128)} %fusion.25), calls=%async_computation.16 | async-start | bytes 262144 | tf_op jit(solution)/shard_map/all_to_all | solution.py:97
  705.5 98.0 %all-reduce.8.cloned.1.call-done = f32[512,128]{1,0:T(8,128)} async-done(((f32[512,128]{1,0:T(8,128)}), f32[512,128]{1,0:T(8,128)}) %all-reduce.8.cloned.1.call-update) | async-done | bytes 262160 | tf_op jit(solution)/shard_map/psum | solution.py:63
  809.9 77.7 %psum.71 = f32[]{:T(128)} all-reduce(f32[]{:T(128)S(6)} %add.187), channel_id=1, replica_groups=mesh['wide'=16,'narrow'=16] {'wide','narrow'}, use_global_device_ids=true, to_apply=%region_35.0 | all-reduce | flops 1 | bytes 8 | tf_op jit(solution)/shard_map/psum | solution.py:157
  (139 shorter events, 135.0 us)
Async XLA Ops:
  7.8 80.3 %copy-start.23 = (s32[32]{0:T(128)}, s32[32]{0:T(128)S(1)}, u32[]{:S(2)}) copy-start(s32[32]{0:T(128)S(1)} %compare_select_fusion.2) | copy-start | bytes 388
  7.8 190.7 %copy-start.22 = (s32[1024]{0:T(1024)}, s32[1024]{0:T(1024)S(1)}, u32[]{:S(2)}) copy-start(s32[1024]{0:T(1024)S(1)} %pad_clamp_fusion.1) | copy-start | bytes 12292
  10.0 17.7 %all-to-all-start.1 = ((bf16[16,2,128]{2,1,0:T(2,128)(2,1)}), bf16[16,2,128]{2,1,0:T(2,128)(2,1)S(1)}, u32[]{:S(2)}, u32[]{:S(2)}) async-start(bf16[16,2,128]{2,1,0:T(2,128)(2,1)} %bitcast.3), calls=%async_computation.1 | async-start | bytes 16384 | tf_op jit(solution)/shard_map/all_to_all | solution.py:70
  18.2 77.7 %copy-start.17 = (s32[256]{0:T(256)}, s32[256]{0:T(256)S(1)}, u32[]{:S(2)}) copy-start(s32[256]{0:T(256)S(1)} %compare_select_fusion.1) | copy-start | bytes 3076
  26.3 179.9 %copy-start.21 = (s32[1024]{0:T(1024)}, s32[1024]{0:T(1024)S(1)}, u32[]{:S(2)}) copy-start(s32[1024]{0:T(1024)S(1)} %pad_clamp_fusion.2) | copy-start | bytes 12292
  27.7 13.2 %all-to-all-start = ((bf16[16,16,128]{2,1,0:T(8,128)(2,1)}), bf16[16,16,128]{2,1,0:T(8,128)(2,1)S(1)}, u32[]{:S(2)}, u32[]{:S(2)}) async-start(bf16[16,16,128]{2,1,0:T(8,128)(2,1)} %bitcast.1), calls=%async_computation | async-start | bytes 131072 | tf_op jit(solution)/shard_map/all_to_all | solution.py:69
  40.9 19.0 %all-to-all-start.2 = ((bf16[16,16,128]{2,1,0:T(8,128)(2,1)}), bf16[16,16,128]{2,1,0:T(8,128)(2,1)S(1)}, u32[]{:S(2)}, u32[]{:S(2)}) async-start(bf16[16,16,128]{2,1,0:T(8,128)(2,1)} %bitcast.6), calls=%async_computation.2 | async-start | bytes 131072 | tf_op jit(solution)/shard_map/all_to_all | solution.py:73
  59.8 202.8 %copy-start.10 = (bf16[16,16,128]{2,1,0:T(8,128)(2,1)}, bf16[16,16,128]{2,1,0:T(8,128)(2,1)S(1)}, u32[]{:S(2)}) copy-start(bf16[16,16,128]{2,1,0:T(8,128)(2,1)S(1)} %all-to-all-done.2) | copy-start | bytes 196612
  74.1 9.9 %all-to-all-start.5 = ((f32[16,2,128]{2,1,0:T(2,128)}), f32[16,2,128]{2,1,0:T(2,128)S(1)}, u32[]{:S(2)}, u32[]{:S(2)}) async-start(f32[16,2,128]{2,1,0:T(2,128)} %bitcast.17), calls=%async_computation.5 | async-start | bytes 32768 | tf_op jit(solution)/shard_map/all_to_all | solution.py:89
  84.0 11.9 %all-to-all-start.3 = ((f32[16,16,128]{2,1,0:T(8,128)}), f32[16,16,128]{2,1,0:T(8,128)S(1)}, u32[]{:S(2)}, u32[]{:S(2)}) async-start(f32[16,16,128]{2,1,0:T(8,128)} %bitcast.11), calls=%async_computation.3 | async-start | bytes 262144 | tf_op jit(solution)/shard_map/all_to_all | solution.py:82
  87.5 110.0 %all-reduce.4.cloned.1.call-start = ((), (), s32[]{:S(2)}) async-start(), calls=%async_computation.18 | async-start | bytes 524288 | tf_op jit(solution)/shard_map/psum | solution.py:63
  89.6 107.9 %copy-start.13 = (f32[512,128]{1,0:T(8,128)S(1)}, f32[512,128]{1,0:T(8,128)}, u32[]{:S(2)}) copy-start(f32[512,128]{1,0:T(8,128)} %param.10) | copy-start | bytes 786436
  198.5 417.0 %copy-start.3 = (f32[512,128]{1,0:T(8,128)}, f32[512,128]{1,0:T(8,128)S(1)}, u32[]{:S(2)}) copy-start(f32[512,128]{1,0:T(8,128)S(1)} %get-tuple-element.20) | copy-start | bytes 786436
  199.7 12.9 %all-to-all-start.7 = ((bf16[16,2,128]{2,1,0:T(2,128)(2,1)}), bf16[16,2,128]{2,1,0:T(2,128)(2,1)S(1)}, u32[]{:S(2)}, u32[]{:S(2)}) async-start(bf16[16,2,128]{2,1,0:T(2,128)(2,1)} %bitcast.21), calls=%async_computation.7 | async-start | bytes 16384 | tf_op jit(solution)/shard_map/all_to_all | solution.py:70
  212.6 10.0 %all-to-all-start.6 = ((bf16[16,16,128]{2,1,0:T(8,128)(2,1)}), bf16[16,16,128]{2,1,0:T(8,128)(2,1)S(1)}, u32[]{:S(2)}, u32[]{:S(2)}) async-start(bf16[16,16,128]{2,1,0:T(8,128)(2,1)} %bitcast.19), calls=%async_computation.6 | async-start | bytes 131072 | tf_op jit(solution)/shard_map/all_to_all | solution.py:69
  222.5 18.5 %all-to-all-start.4 = ((f32[16,16,128]{2,1,0:T(8,128)}), f32[16,16,128]{2,1,0:T(8,128)S(1)}, u32[]{:S(2)}, u32[]{:S(2)}) async-start(f32[16,16,128]{2,1,0:T(8,128)} %fusion.21), calls=%async_computation.4 | async-start | bytes 262144 | tf_op jit(solution)/shard_map/all_to_all | solution.py:97
  244.7 10.8 %all-to-all-start.8 = ((bf16[16,16,128]{2,1,0:T(8,128)(2,1)}), bf16[16,16,128]{2,1,0:T(8,128)(2,1)S(1)}, u32[]{:S(2)}, u32[]{:S(2)}) async-start(bf16[16,16,128]{2,1,0:T(8,128)(2,1)} %bitcast.24), calls=%async_computation.8 | async-start | bytes 131072 | tf_op jit(solution)/shard_map/all_to_all | solution.py:73
  268.3 9.9 %all-to-all-start.11 = ((f32[16,2,128]{2,1,0:T(2,128)}), f32[16,2,128]{2,1,0:T(2,128)S(1)}, u32[]{:S(2)}, u32[]{:S(2)}) async-start(f32[16,2,128]{2,1,0:T(2,128)} %bitcast.34), calls=%async_computation.11 | async-start | bytes 32768 | tf_op jit(solution)/shard_map/all_to_all | solution.py:89
  278.2 13.3 %all-to-all-start.9 = ((f32[16,16,128]{2,1,0:T(8,128)}), f32[16,16,128]{2,1,0:T(8,128)S(1)}, u32[]{:S(2)}, u32[]{:S(2)}) async-start(f32[16,16,128]{2,1,0:T(8,128)} %bitcast.28), calls=%async_computation.9 | async-start | bytes 262144 | tf_op jit(solution)/shard_map/all_to_all | solution.py:82
  284.8 114.7 %all-reduce.6.cloned.1.call-start = ((), (), s32[]{:S(2)}) async-start(), calls=%async_computation.19 | async-start | bytes 524288 | tf_op jit(solution)/shard_map/psum | solution.py:63
  292.3 109.6 %all-to-all-start.10 = ((f32[16,16,128]{2,1,0:T(8,128)}), f32[16,16,128]{2,1,0:T(8,128)}, u32[]{:S(2)}, u32[]{:S(2)}) async-start(f32[16,16,128]{2,1,0:T(8,128)} %fusion.23), calls=%async_computation.10 | async-start | bytes 262144 | tf_op jit(solution)/shard_map/all_to_all | solution.py:97
  619.5 10.4 %all-to-all-start.13 = ((bf16[16,2,128]{2,1,0:T(2,128)(2,1)}), bf16[16,2,128]{2,1,0:T(2,128)(2,1)}, u32[]{:S(2)}, u32[]{:S(2)}) async-start(bf16[16,2,128]{2,1,0:T(2,128)(2,1)} %bitcast.38), calls=%async_computation.13 | async-start | bytes 16384 | tf_op jit(solution)/shard_map/all_to_all | solution.py:70
  629.9 10.7 %all-to-all-start.12 = ((bf16[16,16,128]{2,1,0:T(8,128)(2,1)}), bf16[16,16,128]{2,1,0:T(8,128)(2,1)}, u32[]{:S(2)}, u32[]{:S(2)}) async-start(bf16[16,16,128]{2,1,0:T(8,128)(2,1)} %bitcast.36), calls=%async_computation.12 | async-start | bytes 131072 | tf_op jit(solution)/shard_map/all_to_all | solution.py:69
  640.6 16.8 %all-to-all-start.14 = ((bf16[16,16,128]{2,1,0:T(8,128)(2,1)}), bf16[16,16,128]{2,1,0:T(8,128)(2,1)S(1)}, u32[]{:S(2)}, u32[]{:S(2)}) async-start(bf16[16,16,128]{2,1,0:T(8,128)(2,1)} %bitcast.41), calls=%async_computation.14 | async-start | bytes 131072 | tf_op jit(solution)/shard_map/all_to_all | solution.py:73
  670.1 10.1 %all-to-all-start.17 = ((f32[16,2,128]{2,1,0:T(2,128)}), f32[16,2,128]{2,1,0:T(2,128)S(1)}, u32[]{:S(2)}, u32[]{:S(2)}) async-start(f32[16,2,128]{2,1,0:T(2,128)} %bitcast.49), calls=%async_computation.17 | async-start | bytes 32768 | tf_op jit(solution)/shard_map/all_to_all | solution.py:89
  680.2 13.4 %all-to-all-start.15 = ((f32[16,16,128]{2,1,0:T(8,128)}), f32[16,16,128]{2,1,0:T(8,128)S(1)}, u32[]{:S(2)}, u32[]{:S(2)}) async-start(f32[16,16,128]{2,1,0:T(8,128)} %bitcast.44), calls=%async_computation.15 | async-start | bytes 262144 | tf_op jit(solution)/shard_map/all_to_all | solution.py:82
  686.9 116.6 %all-reduce.8.cloned.1.call-start = ((), (), s32[]{:S(2)}) async-start(), calls=%async_computation.20 | async-start | bytes 524288 | tf_op jit(solution)/shard_map/psum | solution.py:63
  686.9 118.9 %copy-start.16 = (s32[256]{0:T(256)S(1)}, s32[256]{0:T(256)}, u32[]{:S(2)}) copy-start(s32[256]{0:T(256)} %copy-done.14) | copy-start | bytes 3076
  691.1 116.8 %copy-start.5 = (f32[512,128]{1,0:T(8,128)S(1)}, f32[512,128]{1,0:T(8,128)}, u32[]{:S(2)}) copy-start(f32[512,128]{1,0:T(8,128)} %get-tuple-element.16) | copy-start | bytes 786436
  691.1 198.6 %copy-start.4 = (f32[512,128]{1,0:T(8,128)S(1)}, f32[512,128]{1,0:T(8,128)}, u32[]{:S(2)}) copy-start(f32[512,128]{1,0:T(8,128)} %copy-done.3) | copy-start | bytes 786436
  691.1 198.6 %copy-start.7 = (f32[512,128]{1,0:T(8,128)S(1)}, f32[512,128]{1,0:T(8,128)}, u32[]{:S(2)}) copy-start(f32[512,128]{1,0:T(8,128)} %multiply_add_fusion.4) | copy-start | bytes 786436
  693.7 112.1 %all-to-all-start.16 = ((f32[16,16,128]{2,1,0:T(8,128)}), f32[16,16,128]{2,1,0:T(8,128)S(1)}, u32[]{:S(2)}, u32[]{:S(2)}) async-start(f32[16,16,128]{2,1,0:T(8,128)} %fusion.25), calls=%async_computation.16 | async-start | bytes 262144 | tf_op jit(solution)/shard_map/all_to_all | solution.py:97
  (13 other events, 142.0 us)
Sparse Core Ops, SparseCore 0:
  91.3 106.1 all-reduce.3
  290.6 108.8 all-reduce.5
  692.8 110.5 all-reduce.7
